TPU v7x, 128 devices: a whole 4x4x4 slice. The times are simulated.
128 devices in a mesh: expert: 4 (over y), feat: 32 (over x, z, core).
Axes of the slice: x: 4, y: 4, z: 4, core: 2. Of those that a mesh axis runs over, the one named last changes fastest.
Arguments:
- tokens: bfloat16 [1024, 4096], P(('expert', 'feat')), may hold values from -6 to 6
- expert_ids: int32 [1024, 2], P(('expert', 'feat')), may hold values from 0 to 7, as said below
- route_weights: bfloat16 [1024, 2], P(('expert', 'feat')), may hold values from 0.099609375 to 1
- gate_proj: bfloat16 [4096, 28672], P(None, ('expert', 'feat')), may hold values from -0.09375 to 0.09375
- up_proj: bfloat16 [4096, 28672], P(None, ('expert', 'feat')), may hold values from -0.09375 to 0.09375
- down_proj: bfloat16 [28672, 4096], P(('expert', 'feat')), may hold values from -0.046875 to 0.046875
- enc_weight: float32 [4096, 32768], P(None, ('expert', 'feat')), may hold values from -0.09375 to 0.09375
- enc_bias: float32 [32768], P(('expert', 'feat')), may hold values from -3 to 3
- log_threshold: float32 [32768], P(('expert', 'feat')), may hold values from -2.3 to 0
- dec_weight: float32 [32768, 4096], P(('expert', 'feat')), may hold values from -0.046875 to 0.046875
Outputs:
- grad_encoder: float32 [4096, 32768], P(None, ('expert', 'feat'))
- grad_decoder: float32 [32768, 4096], P(('expert', 'feat'))
- grad_bias: float32 [32768], P(('expert', 'feat'))
- grad_threshold: float32 [32768], P(('expert', 'feat'))
Inputs may be any that keep to these rules, and one draw needn't show every extreme that they name: `expert_ids`: each token names two different experts of 0 to 7. Among the 8 tokens of one device, each expert below 2 is named by at most 4 tokens; in every draw one of these experts, drawn from the seed and the same for all devices, is named by exactly 4 tokens of every device.
All inputs are finite; a program needn't handle non-finite values.
Results may differ from a plain program's by a relative error of at most 0.0021.
Values may be sent and summed in bfloat16 or wider, within the bound.
A program may use at most 128 MiB of HBM per device.

v0:
```python
import jax
import jax.numpy as jnp
from jax import lax
from jax.sharding import PartitionSpec as P

sharpness = 0.1
kernel_width = 0.5
density_weight = 0.01
highest = lax.Precision.HIGHEST


def partner(block, axis, stride):
    count = lax.axis_size(axis)
    route = []
    for low in range(count):
        high = low | 1 << stride
        if high != low and high < count:
            route += [(low, high), (high, low)]
    return lax.ppermute(block, axis, route)


def pack_slots(tokens, expert_ids, route_weights, experts):
    capacity = tokens.shape[0] // 2
    window = jnp.arange(experts, dtype=jnp.int32)
    matches = expert_ids[:, :, None] == window[None, None, :]
    named = jnp.sum(matches.astype(jnp.int32), axis=1)
    weighted = jnp.sum(
        jnp.where(matches, route_weights[:, :, None], jnp.zeros((), jnp.bfloat16)), axis=1
    )
    slot_index = jnp.cumsum(named, axis=0) - named
    places = jnp.arange(capacity, dtype=jnp.int32)
    chosen = (named.T[:, None, :] == 1) & (slot_index.T[:, None, :] == places[None, :, None])
    slot_rows = jnp.einsum(
        "ect,td->ecd", chosen.astype(jnp.bfloat16), tokens, preferred_element_type=jnp.float32
    ).astype(jnp.bfloat16)
    slot_weights = jnp.sum(
        jnp.where(chosen, weighted.T[:, None, :], jnp.zeros((), jnp.bfloat16)), axis=2
    )
    return (slot_rows, slot_weights)


def contract_rows(left, right):
    return lax.dot_general(left, right, (((0,), (0,)), ((), ())), precision=highest)


def body(
    tokens,
    expert_ids,
    route_weights,
    gate_proj,
    up_proj,
    down_proj,
    enc_weight,
    enc_bias,
    log_threshold,
    dec_weight,
):
    copies = 2
    experts = lax.axis_size("expert") // copies
    slot_rows, slot_weights = pack_slots(tokens, expert_ids, route_weights, experts)
    send_rows = jnp.repeat(slot_rows, copies, axis=0)
    send_weights = jnp.repeat(slot_weights, copies, axis=0)
    came_rows, came_weights = (
        lax.all_to_all(send_rows, "expert", split_axis=0, concat_axis=0, tiled=True),
        lax.all_to_all(send_weights, "expert", split_axis=0, concat_axis=0, tiled=True),
    )
    all_rows, all_weights = (
        lax.all_gather(came_rows, "feat", axis=0, tiled=True),
        lax.all_gather(came_weights, "feat", axis=0, tiled=True),
    )
    width = tokens.shape[1]
    token_rows = all_rows.reshape(-1, width)
    row_weights = all_weights.reshape(-1).astype(jnp.float32)
    gate_act = jnp.dot(token_rows, gate_proj, preferred_element_type=jnp.float32)
    up_act = jnp.dot(token_rows, up_proj, preferred_element_type=jnp.float32)
    hidden = (jax.nn.silu(gate_act) * up_act).astype(jnp.bfloat16)
    target_part = jnp.dot(hidden, down_proj, preferred_element_type=jnp.float32)
    inputs = token_rows.astype(jnp.float32)
    preact = jnp.dot(inputs, enc_weight, precision=highest) + enc_bias
    threshold = jnp.exp(log_threshold)
    shifted = preact - threshold
    soft_gate = jax.nn.sigmoid(shifted / sharpness)
    active = preact * soft_gate
    partial_error = jnp.dot(active, dec_weight, precision=highest) - target_part
    feat_total = lax.psum(partial_error, "feat")
    recon_error = feat_total + partner(feat_total, "expert", 0)
    residual_grad = 2.0 * row_weights[:, None] * recon_error
    grad_decoder = contract_rows(active, residual_grad)
    grad_active = lax.dot_general(
        residual_grad, dec_weight, (((1,), (1,)), ((), ())), precision=highest
    )
    grad_pre = grad_active * soft_gate
    grad_encoder = contract_rows(inputs, grad_pre)
    grad_bias = jnp.sum(grad_pre, axis=0)
    kernel = jnp.maximum(0.0, 1.0 - jnp.abs(shifted) / kernel_width) / kernel_width
    slope_sum = jnp.sum(
        (grad_active * threshold + density_weight * row_weights[:, None]) * kernel, axis=0
    )
    grad_threshold = -threshold * slope_sum
    return (grad_encoder, grad_decoder, grad_bias, grad_threshold)


def solution(mesh):
    in_specs = (
        P(("expert", "feat"), None),
        P(("expert", "feat"), None),
        P(("expert", "feat"), None),
        P(None, ("expert", "feat")),
        P(None, ("expert", "feat")),
        P(("expert", "feat"), None),
        P(None, ("expert", "feat")),
        P(("expert", "feat")),
        P(("expert", "feat")),
        P(("expert", "feat"), None),
    )
    out_specs = (
        P(None, ("expert", "feat")),
        P(("expert", "feat"), None),
        P(("expert", "feat")),
        P(("expert", "feat")),
    )
    return jax.shard_map(body, mesh=mesh, in_specs=in_specs, out_specs=out_specs, check_vma=False)
```

profile of v0, /device:TPU:1, one launch (start us, length us, event | category | flops | bytes accessed | tf_op | source)
XLA Modules:
  0.0 474.6 jit_solution(3377354966974964132)
XLA Ops:
  7.2 0.0 copy-start
  7.2 0.0 all-gather.3.cloned.1.call-start
  7.2 0.8 convert_reduce_fusion
  8.1 0.2 reduce_window_sum.11
  8.2 1.0 convolution_convert_fusion
  9.3 9.7 %all_to_all.17 = bf16[4,4,4096]{2,1,0:T(4,128)(2,1)} all-to-all(bf16[4,4,4096]{2,1,0:T(4,128)(2,1)S(1)} %bitcast.20), channel_id=1, replica_groups=mesh['expert'=4,'feat'=32] {'expert'}, dimensions={0} | all-to-all | bytes 262144 | tf_op jit(solution)/shard_map/all_to_all | solution.py:64
  19.0 0.0 all-gather.3.cloned.1.call-update
  19.0 0.0 all-reduce.2.cloned.1.call-start
  19.1 0.7 exp.10
  19.8 48.0 %all-gather.3.cloned.1.call-done = bf16[128,4,4096]{2,1,0:T(4,128)(2,1)} async-done(((bf16[4,4,4096]{2,1,0:T(4,128)(2,1)}), bf16[128,4,4096]{2,1,0:T(4,128)(2,1)}) %all-gather.3.cloned.1.call-update) | async-done | bytes 4194320 | tf_op jit(solution)/shard_map/all_gather | solution.py:68
  67.8 6.9 %reshape.45 = bf16[512,4096]{1,0:T(8,128)(2,1)} reshape(bf16[128,4,4096]{2,1,0:T(4,128)(2,1)} %all-gather.3.cloned.1.call-done) | data formatting | bytes 8388608 | tf_op jit(solution)/shard_map/reshape | solution.py:72
  74.7 0.0 copy-start.1
  74.7 0.0 copy-start.7
  74.7 4.3 fusion.31
  79.0 0.0 copy-done.1
  79.0 0.0 copy-done.7
  79.0 5.8 %convolution_add_fusion = f32[512,256]{1,0:T(8,128)S(1)} fusion(bf16[512,4096]{1,0:T(8,128)(2,1)S(1)} %copy-done.1, f32[4096,256]{1,0:T(8,128)} %param.16, f32[256]{0:T(256)S(1)} %copy-done.7), kind=kOutput, calls=%fused_computation.6 | convolution fusion | flops 6442582016 | bytes 8913920 | tf_op jit(solution)/shard_map/dot_general | solution.py:79
  84.9 0.0 copy-done
  84.9 8.7 %fusion.3 = f32[512,4096]{1,0:T(8,128)} fusion(bf16[224,4096]{1,0:T(8,128)(2,1)S(1)} %copy-done, bf16[512,4096]{1,0:T(8,128)(2,1)} %reshape.45, bf16[4096,224]{0,1:T(8,128)(2,1)} %param.14, f32[512,224]{0,1:T(8,128)S(1)} %fusion.31), kind=kOutput, calls=%fused_computation.8 | convolution fusion | flops 1879736320 | bytes 16711680 | tf_op jit(solution)/shard_map/dot_general | solution.py:77
  93.6 13.0 %convolution_subtract_fusion = f32[512,4096]{1,0:T(8,128)} fusion(f32[512,4096]{1,0:T(8,128)} %fusion.3, f32[256,4096]{1,0:T(8,128)} %param.19, f32[512,256]{1,0:T(8,128)S(1)} %convolution_add_fusion, f32[256]{0:T(256)S(1)} %exp.10), kind=kOutput, calls=%fused_computation.1 | convolution fusion | flops 6445334528 | bytes 21496832 | tf_op jit(solution)/shard_map/dot_general | solution.py:84
  106.6 0.0 copy-start.5
  106.6 0.0 copy-start.6
  106.6 0.0 all-reduce.2.cloned.1.call-update
  106.6 119.7 %all-reduce.2.cloned.1.call-done = f32[512,4096]{1,0:T(8,128)} async-done(((f32[512,4096]{1,0:T(8,128)}), f32[512,4096]{1,0:T(8,128)}) %all-reduce.2.cloned.1.call-update) | async-done | bytes 8388624 | tf_op jit(solution)/shard_map/psum | solution.py:85
  226.4 1.2 collective-permute-start
  227.6 0.0 copy-done.5
  227.6 0.0 copy-done.6
  227.6 0.1 fusion.18
  227.7 181.8 %all_to_all.18 = bf16[4,1,4]{2,1,0:T(2,128)(2,1)S(1)} all-to-all(bf16[4,1,4]{2,1,0:T(2,128)(2,1)S(1)} %copy.21), channel_id=1, replica_groups=mesh['expert'=4,'feat'=32] {'expert'}, dimensions={0} | all-to-all | bytes 64 | tf_op jit(solution)/shard_map/all_to_all | solution.py:65
  409.5 26.1 %all-gather = bf16[128,1,4]{2,1,0:T(2,128)(2,1)S(1)} all-gather(bf16[4,1,4]{2,1,0:T(2,128)(2,1)S(1)} %all_to_all.18), channel_id=2, replica_groups=mesh['expert'=4,'feat'=32] {'feat'}, dimensions={0}, use_global_device_ids=true | all-gather | bytes 1056 | tf_op jit(solution)/shard_map/all_gather | solution.py:69
  435.6 0.4 multiply_reduce_fusion.1
  436.0 0.1 mul.73
  436.1 0.1 mul.63
  436.2 0.0 copy-start.2
  436.2 0.0 collective-permute-done
  436.2 13.2 %multiply_reduce_fusion = (f32[256]{0:T(256)S(1)}, f32[256]{0:T(256)}, f32[512,256]{1,0:T(8,128)S(1)}) fusion(f32[512,256]{1,0:T(8,128)S(1)} %convolution_add_fusion, f32[512]{0:T(512)S(1)} %mul.73, f32[256]{0:T(256)S(1)} %exp.10, f32[256,4096]{1,0:T(8,128)} %param.19, f32[512,4096]{1,0:T(8,128)} %all-reduce.2.cloned.1.call-done, ...), kind=kOutput, calls=%fused_computation.9 | convolution fusion | flops 6448741888 | bytes 22027264 | tf_op jit(solution)/shard_map/dot_general | solution.py:89
  449.4 0.0 copy-done.2
  449.4 0.0 copy-start.4
  449.4 0.0 copy-start.3
  449.4 6.3 %fusion.29 = f32[4096,256]{1,0:T(8,128)} fusion(bf16[512,4096]{1,0:T(8,128)(2,1)S(1)} %copy-done.2, f32[512,256]{1,0:T(8,128)S(1)} %get-tuple-element.8, f32[512,256]{1,0:T(8,128)S(1)} %convolution_add_fusion, f32[256]{0:T(256)S(1)} %exp.10), kind=kOutput, calls=%fused_computation.41 | convolution fusion | flops 6443237376 | bytes 9438208 | tf_op jit(solution)/shard_map/dot_general | solution.py:43
  455.7 0.0 copy-done.4
  455.7 0.6 negate_multiply_fusion
  456.3 0.0 copy-done.3
  456.3 11.5 %fusion = f32[256,4096]{1,0:T(8,128)} fusion(f32[512,4096]{1,0:T(8,128)S(1)} %copy-done.3, f32[512,4096]{1,0:T(8,128)} %collective-permute-done, f32[512]{0:T(512)S(1)} %mul.63, f32[512,256]{1,0:T(8,128)S(1)} %convolution_add_fusion, f32[256]{0:T(256)S(1)} %exp.10), kind=kOutput, calls=%fused_computation.4 | convolution fusion | flops 6447431680 | bytes 21498880 | tf_op jit(solution)/shard_map/dot_general | solution.py:43
  (6 shorter events, 0.1 us)
Async XLA Ops:
  7.2 77.7 %copy-start = (bf16[224,4096]{1,0:T(8,128)(2,1)S(1)}, bf16[224,4096]{1,0:T(8,128)(2,1)}, u32[]{:S(2)}) copy-start(bf16[224,4096]{1,0:T(8,128)(2,1)} %param.15) | copy-start | bytes 5505028
  7.2 60.6 %all-gather.3.cloned.1.call-start = ((), (), s32[]{:S(2)}) async-start(), calls=%async_computation.2 | async-start | bytes 4325376 | tf_op jit(solution)/shard_map/all_gather | solution.py:68
  19.0 207.3 %all-reduce.2.cloned.1.call-start = ((), (), s32[]{:S(2)}) async-start(), calls=%async_computation.3 | async-start | bytes 16777216 | tf_op jit(solution)/shard_map/psum | solution.py:85
  74.7 4.4 copy-start.1
  74.7 4.4 copy-start.7
  106.6 121.0 %copy-start.5 = (s32[8,2]{0,1:T(2,128)S(1)}, s32[8,2]{0,1:T(2,128)}, u32[]{:S(2)}) copy-start(s32[8,2]{0,1:T(2,128)} %param.11) | copy-start | bytes 196
  106.6 121.0 %copy-start.6 = (bf16[8,2]{0,1:T(2,128)(2,1)S(1)}, bf16[8,2]{0,1:T(2,128)(2,1)}, u32[]{:S(2)}) copy-start(bf16[8,2]{0,1:T(2,128)(2,1)} %param.12) | copy-start | bytes 100
  226.4 209.8 %collective-permute-start = (f32[512,4096]{1,0:T(8,128)}, f32[512,4096]{1,0:T(8,128)}, u32[]{:S(2)}, u32[]{:S(2)}) collective-permute-start(f32[512,4096]{1,0:T(8,128)} %all-reduce.2.cloned.1.call-done), channel_id=1, source_target_pairs={{0,32},{32,0},{64,96},{96,64},{1,33},{33,1},{65,97},{97,65},{2,34}... | collective-permute-start | bytes 25165832 | tf_op jit(solution)/shard_map/ppermute | solution.py:19
  436.2 13.2 %copy-start.2 = (bf16[512,4096]{1,0:T(8,128)(2,1)S(1)}, bf16[512,4096]{1,0:T(8,128)(2,1)}, u32[]{:S(2)}) copy-start(bf16[512,4096]{1,0:T(8,128)(2,1)} %reshape.45) | copy-start | bytes 12582916
  449.4 6.3 %copy-start.4 = (f32[256]{0:T(256)S(1)}, f32[256]{0:T(256)}, u32[]{:S(2)}) copy-start(f32[256]{0:T(256)} %param.18) | copy-start | bytes 3076
  449.4 6.9 %copy-start.3 = (f32[512,4096]{1,0:T(8,128)S(1)}, f32[512,4096]{1,0:T(8,128)}, u32[]{:S(2)}) copy-start(f32[512,4096]{1,0:T(8,128)} %all-reduce.2.cloned.1.call-done) | copy-start | bytes 25165828
Sparse Core Ops, SparseCore 0:
  19.2 48.5 all-gather.2
  106.8 119.5 all-reduce.1
where the time goes:
time: 475 us
  blocking collectives  218 us (46%)
  waiting for transfers between devices  168 us (35%)
  matrix products  63.9 us (13%)
  between operations  14.1 us (3%)
  local copies, waits for them, and re-layouts  7.86 us (2%)
    all_to_all x1, blocking collectives, body(): lax.all_to_all(send_weights, 'expert', split_axis=0, concat_axis=0, tiled...  182 us
    psum x1, waiting for transfers between devices, body(): feat_total = lax.psum(partial_error, 'feat')  120 us
    all_gather x1, waiting for transfers between devices, body(): lax.all_gather(came_rows, 'feat', axis=0, tiled=True)  48 us
    all_gather x1, blocking collectives, body(): lax.all_gather(came_weights, 'feat', axis=0, tiled=True)  26.1 us
    dot_general x2, matrix products, contract_rows(): lax.dot_general(left, right, (((0,), (0,)), ((), ())), precision=highest)  17.8 us
    dot_general x1, matrix products, body(): lax.dot_general(residual_grad, dec_weight, (((1,), (1,)), ((), ())), prec...  13.2 us
    dot_general x1, matrix products, body(): partial_error = jnp.dot(active, dec_weight, precision=highest) - target_part  13 us
    all_to_all x1, blocking collectives, body(): lax.all_to_all(send_rows, 'expert', split_axis=0, concat_axis=0, tiled=True)  9.75 us
  transfers between devices with their start and end apart: 3, of which 2 were waited for; matrix products, arithmetic and copies ran while one was open for 0% of the time, Pallas kernels for 0%

commit v1 on v0

--- a/solution.py
+++ b/solution.py
@@ -82,7 +82,12 @@
     soft_gate = jax.nn.sigmoid(shifted / sharpness)
     active = preact * soft_gate
     partial_error = jnp.dot(active, dec_weight, precision=highest) - target_part
-    feat_total = lax.psum(partial_error, "feat")
+    world_n = lax.axis_size("feat")
+    feat_total = partial_error
+    for i0 in [hop_no for hop_no in (1, 2, 4, 8, 16) if hop_no < world_n]:
+        feat_total = feat_total + lax.ppermute(
+            feat_total, axis_name="feat", perm=[(u, u ^ i0) for u in range(world_n)]
+        )
     recon_error = feat_total + partner(feat_total, "expert", 0)
     residual_grad = 2.0 * row_weights[:, None] * recon_error
     grad_decoder = contract_rows(active, residual_grad)

time: 475 us -> 1150 us (2.42)
  waiting for transfers between devices: 168 us -> 782 us
  other arithmetic: 2.08 us -> 57.7 us
    ppermute x0 -> x5, waiting for transfers between devices: none -> 733 us  [body(): lax.ppermute(feat_total, axis_name='feat', perm=[(u, u ^ i0) for u in ran...]
    psum x1 -> x0, waiting for transfers between devices: 120 us -> none  [body(): feat_total = lax.psum(partial_error, 'feat')]
    add x0 -> x5, other arithmetic: none -> 55.7 us  [body(): feat_total + lax.ppermute(feat_total, axis_name='feat', perm=[(u, u ^ i0)...]
  transfers between devices with their start and end apart: 3 -> 7, of which waited for: 2 -> 6; matrix products, arithmetic and copies ran while one was open for 0% -> 0% of each run, Pallas kernels for 0% -> 0%
where the time goes in v1:
time: 1150 us
  waiting for transfers between devices  782 us (68%)
  blocking collectives  217 us (19%)
  matrix products  61.6 us (5%)
  other arithmetic  57.7 us (5%)
  between operations  14.1 us (1%)
    ppermute x5, waiting for transfers between devices, body(): lax.ppermute(feat_total, axis_name='feat', perm=[(u, u ^ i0) for u in ran...  733 us
    all_to_all x1, blocking collectives, body(): lax.all_to_all(send_weights, 'expert', split_axis=0, concat_axis=0, tiled...  179 us
    add x5, other arithmetic, body(): feat_total + lax.ppermute(feat_total, axis_name='feat', perm=[(u, u ^ i0)...  55.7 us
    all_gather x1, waiting for transfers between devices, body(): lax.all_gather(came_rows, 'feat', axis=0, tiled=True)  48.1 us
    all_gather x1, blocking collectives, body(): lax.all_gather(came_weights, 'feat', axis=0, tiled=True)  28.6 us
  transfers between devices with their start and end apart: 7, of which 6 were waited for; matrix products, arithmetic and copies ran while one was open for 0% of the time, Pallas kernels for 0%

profile of v1, /device:TPU:1, one launch (start us, length us, event | category | flops | bytes accessed | tf_op | source)
XLA Modules:
  0.0 1150.2 jit_solution(7684335809899829852)
XLA Ops:
  7.2 0.0 copy-start
  7.2 0.0 all-gather.3.cloned.1.call-start
  7.2 0.8 convert_reduce_fusion
  8.1 0.2 reduce_window_sum.11
  8.2 1.0 convolution_convert_fusion
  9.3 9.7 all_to_all.17
  19.0 0.0 all-gather.3.cloned.1.call-update
  19.1 0.7 exp.10
  19.7 48.1 %all-gather.3.cloned.1.call-done = bf16[128,4,4096]{2,1,0:T(4,128)(2,1)} async-done(((bf16[4,4,4096]{2,1,0:T(4,128)(2,1)}), bf16[128,4,4096]{2,1,0:T(4,128)(2,1)}) %all-gather.3.cloned.1.call-update) | async-done | bytes 4194320 | tf_op jit(solution)/shard_map/all_gather | solution.py:68
  67.8 6.9 reshape.45
  74.7 4.3 fusion.31
  79.0 0.0 copy-done.3
  79.0 0.0 copy-done.9
  79.0 5.8 convolution_add_fusion
  84.9 8.7 fusion.3
  93.6 10.6 convolution_subtract_fusion
  104.2 3.2 copy-done.5
  107.4 0.3 collective-permute-start
  107.7 13.0 %collective-permute-done = f32[512,4096]{1,0:T(8,128)} collective-permute-done((f32[512,4096]{1,0:T(8,128)S(1)}, f32[512,4096]{1,0:T(8,128)}, u32[]{:S(2)}, u32[]{:S(2)}) %collective-permute-start) | collective-permute-done | bytes 8388640 | tf_op jit(solution)/shard_map/ppermute | solution.py:88
  120.7 11.1 add.45
  131.8 0.9 collective-permute-start.1
  132.7 181.2 %collective-permute-done.1 = f32[512,4096]{1,0:T(8,128)} collective-permute-done((f32[512,4096]{1,0:T(8,128)}, f32[512,4096]{1,0:T(8,128)}, u32[]{:S(2)}, u32[]{:S(2)}) %collective-permute-start.1) | collective-permute-done | bytes 8388640 | tf_op jit(solution)/shard_map/ppermute | solution.py:88
  314.0 11.1 add.46
  325.1 2.1 collective-permute-start.2
  327.2 180.6 %collective-permute-done.2 = f32[512,4096]{1,0:T(8,128)} collective-permute-done((f32[512,4096]{1,0:T(8,128)}, f32[512,4096]{1,0:T(8,128)}, u32[]{:S(2)}, u32[]{:S(2)}) %collective-permute-start.2) | collective-permute-done | bytes 8388640 | tf_op jit(solution)/shard_map/ppermute | solution.py:88
  507.8 11.1 add.47
  518.9 0.7 collective-permute-start.3
  519.6 179.6 %collective-permute-done.3 = f32[512,4096]{1,0:T(8,128)} collective-permute-done((f32[512,4096]{1,0:T(8,128)}, f32[512,4096]{1,0:T(8,128)}, u32[]{:S(2)}, u32[]{:S(2)}) %collective-permute-start.3) | collective-permute-done | bytes 8388640 | tf_op jit(solution)/shard_map/ppermute | solution.py:88
  699.2 11.1 add.48
  710.3 1.8 collective-permute-start.4
  712.1 179.1 %collective-permute-done.4 = f32[512,4096]{1,0:T(8,128)} collective-permute-done((f32[512,4096]{1,0:T(8,128)}, f32[512,4096]{1,0:T(8,128)}, u32[]{:S(2)}, u32[]{:S(2)}) %collective-permute-start.4) | collective-permute-done | bytes 8388640 | tf_op jit(solution)/shard_map/ppermute | solution.py:88
  891.2 11.1 add.49
  902.3 1.2 collective-permute-start.5
  903.6 0.0 copy-done.8
  903.6 0.1 fusion.18
  903.7 178.7 %all_to_all.18 = bf16[4,1,4]{2,1,0:T(2,128)(2,1)S(1)} all-to-all(bf16[4,1,4]{2,1,0:T(2,128)(2,1)S(1)} %copy.21), channel_id=1, replica_groups=mesh['expert'=4,'feat'=32] {'expert'}, dimensions={0} | all-to-all | bytes 64 | tf_op jit(solution)/shard_map/all_to_all | solution.py:65
  1082.4 28.6 %all-gather = bf16[128,1,4]{2,1,0:T(2,128)(2,1)S(1)} all-gather(bf16[4,1,4]{2,1,0:T(2,128)(2,1)S(1)} %all_to_all.18), channel_id=2, replica_groups=mesh['expert'=4,'feat'=32] {'feat'}, dimensions={0}, use_global_device_ids=true | all-gather | bytes 1056 | tf_op jit(solution)/shard_map/all_gather | solution.py:69
  1111.0 0.4 multiply_reduce_fusion.1
  1111.4 0.1 mul.73
  1111.5 0.1 mul.63
  1111.6 0.0 copy-start.4
  1111.6 0.0 collective-permute-done.5
  1111.6 13.2 %multiply_reduce_fusion = (f32[256]{0:T(256)S(1)}, f32[256]{0:T(256)}, f32[512,256]{1,0:T(8,128)S(1)}) fusion(f32[512,256]{1,0:T(8,128)S(1)} %convolution_add_fusion, f32[512]{0:T(512)S(1)} %mul.73, f32[256]{0:T(256)S(1)} %exp.10, f32[256,4096]{1,0:T(8,128)} %param.19, f32[512,4096]{1,0:T(8,128)} %add.49, f32[512,4096]{1,0:T(8,128)} %collective-permute-done.5, ...), kind=kOutput, calls=%fused_computation.9 | convolution fusion | flops 6448741888 | bytes 22027264 | tf_op jit(solution)/shard_map/dot_general | solution.py:94
  1124.8 0.0 copy-done.4
  1124.8 6.3 fusion.29
  1131.1 0.6 negate_multiply_fusion
  1131.7 0.0 copy-done.2
  1131.7 11.6 %fusion = f32[256,4096]{1,0:T(8,128)} fusion(f32[512,4096]{1,0:T(8,128)S(1)} %copy-done.2, f32[512,4096]{1,0:T(8,128)} %collective-permute-done.5, f32[512]{0:T(512)S(1)} %mul.63, f32[512,256]{1,0:T(8,128)S(1)} %convolution_add_fusion, f32[256]{0:T(256)S(1)} %exp.10), kind=kOutput, calls=%fused_computation.4 | convolution fusion | flops 6447431680 | bytes 21498880 | tf_op jit(solution)/shard_map/dot_general | solution.py:43
  (18 shorter events, 0.1 us)
Async XLA Ops:
  7.2 77.7 %copy-start = (bf16[224,4096]{1,0:T(8,128)(2,1)S(1)}, bf16[224,4096]{1,0:T(8,128)(2,1)}, u32[]{:S(2)}) copy-start(bf16[224,4096]{1,0:T(8,128)(2,1)} %param.15) | copy-start | bytes 5505028
  7.2 60.6 %all-gather.3.cloned.1.call-start = ((), (), s32[]{:S(2)}) async-start(), calls=%async_computation.2 | async-start | bytes 4325376 | tf_op jit(solution)/shard_map/all_gather | solution.py:68
  74.7 4.3 copy-start.3
  74.7 4.4 copy-start.9
  104.2 3.2 copy-start.5
  107.4 13.3 %collective-permute-start = (f32[512,4096]{1,0:T(8,128)S(1)}, f32[512,4096]{1,0:T(8,128)}, u32[]{:S(2)}, u32[]{:S(2)}) collective-permute-start(f32[512,4096]{1,0:T(8,128)S(1)} %convolution_subtract_fusion), channel_id=1, source_target_pairs={{0,1},{1,0},{2,3},{3,2},{4,5},{5,4},{6,7},{7,6},{8,9},{9,8},{10,11... | collective-permute-start | bytes 25165832 | tf_op jit(solution)/shard_map/ppermute | solution.py:88
  131.8 182.1 %collective-permute-start.1 = (f32[512,4096]{1,0:T(8,128)}, f32[512,4096]{1,0:T(8,128)}, u32[]{:S(2)}, u32[]{:S(2)}) collective-permute-start(f32[512,4096]{1,0:T(8,128)} %add.45), channel_id=1, source_target_pairs={{0,2},{1,3},{2,0},{3,1},{4,6},{5,7},{6,4},{7,5},{8,10},{9,11},{10,... | collective-permute-start | bytes 25165832 | tf_op jit(solution)/shard_map/ppermute | solution.py:88
  325.1 182.7 %collective-permute-start.2 = (f32[512,4096]{1,0:T(8,128)}, f32[512,4096]{1,0:T(8,128)}, u32[]{:S(2)}, u32[]{:S(2)}) collective-permute-start(f32[512,4096]{1,0:T(8,128)} %add.46), channel_id=1, source_target_pairs={{0,4},{1,5},{2,6},{3,7},{4,0},{5,1},{6,2},{7,3},{8,12},{9,13},{10,... | collective-permute-start | bytes 25165832 | tf_op jit(solution)/shard_map/ppermute | solution.py:88
  518.9 180.3 %collective-permute-start.3 = (f32[512,4096]{1,0:T(8,128)}, f32[512,4096]{1,0:T(8,128)}, u32[]{:S(2)}, u32[]{:S(2)}) collective-permute-start(f32[512,4096]{1,0:T(8,128)} %add.47), channel_id=1, source_target_pairs={{0,8},{1,9},{2,10},{3,11},{4,12},{5,13},{6,14},{7,15},{8,0},{9,1},... | collective-permute-start | bytes 25165832 | tf_op jit(solution)/shard_map/ppermute | solution.py:88
  710.3 193.2 %copy-start.7 = (s32[8,2]{0,1:T(2,128)S(1)}, s32[8,2]{0,1:T(2,128)}, u32[]{:S(2)}) copy-start(s32[8,2]{0,1:T(2,128)} %param.11) | copy-start | bytes 196
  710.3 193.2 %copy-start.8 = (bf16[8,2]{0,1:T(2,128)(2,1)S(1)}, bf16[8,2]{0,1:T(2,128)(2,1)}, u32[]{:S(2)}) copy-start(bf16[8,2]{0,1:T(2,128)(2,1)} %param.12) | copy-start | bytes 100
  710.3 180.9 %collective-permute-start.4 = (f32[512,4096]{1,0:T(8,128)}, f32[512,4096]{1,0:T(8,128)}, u32[]{:S(2)}, u32[]{:S(2)}) collective-permute-start(f32[512,4096]{1,0:T(8,128)} %add.48), channel_id=1, source_target_pairs={{0,16},{1,17},{2,18},{3,19},{4,20},{5,21},{6,22},{7,23},{8,24},{9,... | collective-permute-start | bytes 25165832 | tf_op jit(solution)/shard_map/ppermute | solution.py:88
  902.3 209.3 %collective-permute-start.5 = (f32[512,4096]{1,0:T(8,128)}, f32[512,4096]{1,0:T(8,128)}, u32[]{:S(2)}, u32[]{:S(2)}) collective-permute-start(f32[512,4096]{1,0:T(8,128)} %add.49), channel_id=1, source_target_pairs={{0,32},{32,0},{64,96},{96,64},{1,33},{33,1},{65,97},{97,65},{2,34}... | collective-permute-start | bytes 25165832 | tf_op jit(solution)/shard_map/ppermute | solution.py:19
  1111.6 13.2 %copy-start.4 = (bf16[512,4096]{1,0:T(8,128)(2,1)S(1)}, bf16[512,4096]{1,0:T(8,128)(2,1)}, u32[]{:S(2)}) copy-start(bf16[512,4096]{1,0:T(8,128)(2,1)} %reshape.45) | copy-start | bytes 12582916
  1124.8 6.3 copy-start.6
  1124.8 6.9 copy-start.2
  1131.7 11.7 %copy-start.1 = (bf16[224,4096]{1,0:T(8,128)(2,1)S(1)}, bf16[224,4096]{1,0:T(8,128)(2,1)}, u32[]{:S(2)}) copy-start(bf16[224,4096]{1,0:T(8,128)(2,1)} %param.15) | copy-start | bytes 5505028
Sparse Core Ops, SparseCore 0:
  19.2 48.5 all-gather.2
